TPU v7x, 32 devices: a whole 2x2x4 slice. The times are simulated.
32 devices in a mesh: row: 4 (over y, core), col: 8 (over z, x).
Axes of the slice: x: 2, y: 2, z: 4, core: 2. Of those that a mesh axis runs over, the one named last changes fastest.
Arguments:
- row_points: float32 [64, 8192], P(None, 'row'), may hold values from -6 to 6
- panel_points: float32 [64, 1024], P(None, 'col'), may hold values from -6 to 6
- scales: float32 [64], replicated, may hold values from 0.005 to 0.03
Outputs:
- diag_factor: float32 [1024, 1024], P('row', 'col')
- panel_factor_t: float32 [1024, 8192], P('col', 'row')
- updated_ahead_t: float32 [1024, 8192], P('col', 'row')
All inputs are finite; a program needn't handle non-finite values.
Results may differ from a plain program's by a relative error of at most 0.0003.
Values sent between devices are 32-bit elements; how exact they have to be, the bound alone decides.
A program may use at most 128 MiB of HBM per device.

v0:
```python
import jax
import jax.numpy as jnp
from jax import lax
from jax.sharding import PartitionSpec as P

B = 1024


RIDGE = 0.5


def spread(block, axis, holder):
    block = jnp.where(lax.axis_index(axis) == holder, block, jnp.zeros_like(block))
    return lax.psum(block, axis)


def kernel_block(sources, targets, scales):
    weighted = sources * scales[:, None]
    source_sq = jnp.sum(weighted * sources, axis=0)
    target_sq = jnp.sum(targets * targets * scales[:, None], axis=0)
    cross = lax.dot_general(
        weighted,
        targets,
        (((0,), (0,)), ((), ())),
        precision=lax.Precision.HIGHEST,
        preferred_element_type=jnp.float32,
    )
    return jnp.exp(2.0 * cross - source_sq[:, None] - target_sq[None, :])


def times_left(matrix, pieces):
    return jnp.dot(
        matrix, pieces, precision=lax.Precision.HIGHEST, preferred_element_type=jnp.float32
    )


def transposed_times(matrix, pieces):
    return lax.dot_general(
        matrix,
        pieces,
        (((0,), (0,)), ((), ())),
        precision=lax.Precision.HIGHEST,
        preferred_element_type=jnp.float32,
    )


def body(row_points, panel_points, scales):
    n_col = lax.axis_size("col")
    n_row = lax.axis_size("row")
    col_index = lax.axis_index("col")
    row_index = lax.axis_index("row")
    col_share = B // n_col
    row_share = B // n_row
    rows_dev = row_points.shape[1]
    all_panel = lax.all_gather(panel_points, "col", axis=1, tiled=True)
    first_col = col_index * col_share
    root_row = first_col // rows_dev
    local_look = lax.dynamic_slice_in_dim(row_points, first_col % rows_dev, col_share, 1)
    look_points = spread(local_look, "row", root_row)
    identity = jnp.eye(B, dtype=jnp.float32)
    diag_block = kernel_block(all_panel, all_panel, scales) + RIDGE * identity
    diag_full = jnp.linalg.cholesky(diag_block)
    inverse = lax.linalg.triangular_solve(diag_full, identity, left_side=True, lower=True)
    own_inverse = lax.dynamic_slice_in_dim(inverse, first_col, col_share, 0)
    look_kernel = kernel_block(all_panel, look_points, scales)
    look_factor = times_left(inverse, look_kernel)
    look_rows = kernel_block(look_points, row_points, scales)
    own_kernel = kernel_block(panel_points, row_points, scales)
    panel_tile = times_left(own_inverse, lax.all_gather(own_kernel, "col", axis=0, tiled=True))
    reduction = transposed_times(look_factor, lax.all_gather(panel_tile, "col", axis=0, tiled=True))
    updated = look_rows - reduction
    diag_tile = lax.dynamic_slice(
        diag_full, (row_index * row_share, first_col), (row_share, col_share)
    )
    return (diag_tile, panel_tile, updated)


def solution(mesh):
    return jax.shard_map(
        body,
        mesh=mesh,
        in_specs=(P(None, "row"), P(None, "col"), P()),
        out_specs=(P("row", "col"), P("col", "row"), P("col", "row")),
        check_vma=False,
    )
```

profile of v0, /device:TPU:0, one launch (start us, length us, event | category | flops | bytes accessed | tf_op | source)
XLA Modules:
  0.0 574.7 jit_solution(14959280216205739915)
XLA Ops:
  8.0 12.9 %psum.7 = f32[64,128]{1,0:T(8,128)S(1)} all-reduce(f32[64,128]{1,0:T(8,128)S(1)} %dynamic-slice_select_fusion), channel_id=1, replica_groups=mesh['row'=4,'col'=8] {'row'}, use_global_device_ids=true, to_apply=%region_20.21 | all-reduce | flops 8192 | bytes 65536 | tf_op jit(solution)/shard_map/psum | solution.py:14
  22.9 3.3 fusion.8
  26.3 32.4 %all_gather.9 = f32[64,1024]{1,0:T(8,128)S(1)} all-gather(f32[64,128]{1,0:T(8,128)} %param.4), channel_id=1, replica_groups=mesh['row'=4,'col'=8] {'col'}, dimensions={1}, use_global_device_ids=true | all-gather | bytes 294912 | tf_op jit(solution)/shard_map/all_gather | solution.py:55
  59.5 5.8 %fusion.46 = f32[1024,1024]{1,0:T(8,128)} fusion(f32[64,1024]{1,0:T(8,128)S(1)} %all_gather.9, f32[64]{0:T(128)} %param.5), kind=kOutput, calls=%fused_computation.74 | convolution fusion | flops 805371904 | bytes 4456704 | tf_op jit(solution)/shard_map/dot_general | solution.py:21
  65.3 4.9 fusion.1
  70.2 5.4 copy.6
  75.5 5.3 add_multiply_fusion
  82.8 11.7 %cholesky.222 = f32[128,128]{1,0:T(8,128)S(1)} custom-call(f32[128,128]{1,0:T(8,128)S(1)} %cholesky.577), custom_call_target="Cholesky" | custom-call | tf_op jit(solution)/shard_map/jit(cholesky)/cholesky | solution.py:62
  94.5 9.8 %custom-call.62 = f32[1,128,128]{1,2,0:T(8,128)S(1)} custom-call(f32[1,128,128]{2,1,0:T(8,128)S(1)} %get-tuple-element.74), custom_call_target="InvertDiagBlocksLowerTriangular" | custom-call | tf_op jit(solution)/shard_map/jit(cholesky)/cholesky | solution.py:62
  104.4 2.5 cholesky.254
  106.8 2.3 constant_dynamic-update-slice_fusion.31
  110.7 11.7 %cholesky.243 = f32[128,128]{1,0:T(8,128)S(1)} custom-call(f32[128,128]{1,0:T(8,128)S(1)} %cholesky.581), custom_call_target="Cholesky" | custom-call | tf_op jit(solution)/shard_map/jit(cholesky)/cholesky | solution.py:62
  123.1 9.9 %custom-call.63 = f32[1,128,128]{1,2,0:T(8,128)S(1)} custom-call(f32[1,128,128]{2,1,0:T(8,128)S(1)} %get-tuple-element.71), custom_call_target="InvertDiagBlocksLowerTriangular" | custom-call | tf_op jit(solution)/shard_map/jit(cholesky)/cholesky | solution.py:62
  134.3 2.1 convolution_subtract_fusion.6
  136.4 11.7 %cholesky.466 = f32[128,128]{1,0:T(8,128)S(1)} custom-call(f32[128,128]{1,0:T(8,128)S(1)} %cholesky.586), custom_call_target="Cholesky" | custom-call | tf_op jit(solution)/shard_map/jit(cholesky)/cholesky | solution.py:62
  148.8 9.8 %custom-call.64 = f32[1,128,128]{1,2,0:T(8,128)S(1)} custom-call(f32[1,128,128]{2,1,0:T(8,128)S(1)} %get-tuple-element.68), custom_call_target="InvertDiagBlocksLowerTriangular" | custom-call | tf_op jit(solution)/shard_map/jit(cholesky)/cholesky | solution.py:62
  159.8 2.3 convolution_subtract_fusion.7
  162.1 11.9 %cholesky.485 = f32[128,128]{1,0:T(8,128)S(1)} custom-call(f32[128,128]{1,0:T(8,128)S(1)} %cholesky.591), custom_call_target="Cholesky" | custom-call | tf_op jit(solution)/shard_map/jit(cholesky)/cholesky | solution.py:62
  174.7 9.8 %custom-call.65 = f32[1,128,128]{1,2,0:T(8,128)S(1)} custom-call(f32[1,128,128]{2,1,0:T(8,128)S(1)} %get-tuple-element.65), custom_call_target="InvertDiagBlocksLowerTriangular" | custom-call | tf_op jit(solution)/shard_map/jit(cholesky)/cholesky | solution.py:62
  185.6 2.3 convolution_subtract_fusion.8
  188.0 11.7 %cholesky.504 = f32[128,128]{1,0:T(8,128)S(1)} custom-call(f32[128,128]{1,0:T(8,128)S(1)} %cholesky.596), custom_call_target="Cholesky" | custom-call | tf_op jit(solution)/shard_map/jit(cholesky)/cholesky | solution.py:62
  200.3 9.8 %custom-call.66 = f32[1,128,128]{1,2,0:T(8,128)S(1)} custom-call(f32[1,128,128]{2,1,0:T(8,128)S(1)} %get-tuple-element.62), custom_call_target="InvertDiagBlocksLowerTriangular" | custom-call | tf_op jit(solution)/shard_map/jit(cholesky)/cholesky | solution.py:62
  211.1 2.7 convolution_subtract_fusion.9
  213.9 11.7 %cholesky.524 = f32[128,128]{1,0:T(8,128)S(1)} custom-call(f32[128,128]{1,0:T(8,128)S(1)} %cholesky.601), custom_call_target="Cholesky" | custom-call | tf_op jit(solution)/shard_map/jit(cholesky)/cholesky | solution.py:62
  226.2 9.8 %custom-call.67 = f32[1,128,128]{1,2,0:T(8,128)S(1)} custom-call(f32[1,128,128]{2,1,0:T(8,128)S(1)} %get-tuple-element.59), custom_call_target="InvertDiagBlocksLowerTriangular" | custom-call | tf_op jit(solution)/shard_map/jit(cholesky)/cholesky | solution.py:62
  239.1 11.7 %cholesky.544 = f32[128,128]{1,0:T(8,128)S(1)} custom-call(f32[128,128]{1,0:T(8,128)S(1)} %cholesky.606), custom_call_target="Cholesky" | custom-call | tf_op jit(solution)/shard_map/jit(cholesky)/cholesky | solution.py:62
  251.4 9.9 %custom-call.68 = f32[1,128,128]{1,2,0:T(8,128)S(1)} custom-call(f32[1,128,128]{2,1,0:T(8,128)S(1)} %get-tuple-element.56), custom_call_target="InvertDiagBlocksLowerTriangular" | custom-call | tf_op jit(solution)/shard_map/jit(cholesky)/cholesky | solution.py:62
  264.0 11.7 %cholesky.562 = f32[128,128]{1,0:T(8,128)S(1)} custom-call(f32[128,128]{1,0:T(8,128)S(1)} %convolution_subtract_fusion.11), custom_call_target="Cholesky" | custom-call | tf_op jit(solution)/shard_map/jit(cholesky)/cholesky | solution.py:62
  286.1 6.6 %fusion = (f32[1024,1024]{1,0:T(8,128)}, f32[1024,1024]{1,0:T(8,128)}) fusion(f32[1024,1024]{1,0:T(8,128)} %get-tuple-element.54, pred[]{:T(512)S(6)} %cholesky.576), kind=kLoop, calls=%fused_computation.8 | loop fusion | flops 4194304 | bytes 12582913 | tf_op jit(solution)/shard_map/triangular_solve | solution.py:63
  292.7 23.2 %while.1 = (s32[]{:T(128)}, f32[1024,1024]{1,0:T(8,128)}, s32[8,2]{0,1:T(2,128)S(1)}, f32[8,128,128]{2,1,0:T(8,128)S(1)}, s32[]{:T(128)}) while((s32[]{:T(128)}, f32[1024,1024]{1,0:T(8,128)}, s32[8,2]{0,1:T(2,128)S(1)}, f32[8,128,128]{2,1,0:T(8,128)S(1)}, s32[]{:T(128)}) %tuple.65), condition=%wide.while_cond, body=%wide.while_body.sunk | while | flops 2 | bytes 131181 | solution.py:63
  293.3 2.3 bitcast_dynamic-update-slice_fusion.2
  296.2 2.3 bitcast_dynamic-update-slice_fusion.2
  299.1 2.3 bitcast_dynamic-update-slice_fusion.2
  302.0 2.3 bitcast_dynamic-update-slice_fusion.2
  304.9 2.3 bitcast_dynamic-update-slice_fusion.2
  307.8 2.3 bitcast_dynamic-update-slice_fusion.2
  310.7 2.3 bitcast_dynamic-update-slice_fusion.2
  313.6 2.2 bitcast_dynamic-update-slice_fusion.2
  315.9 78.8 %custom-call.69 = f32[8,128,128]{1,2,0:T(8,128)S(1)} custom-call(f32[8,128,128]{2,1,0:T(8,128)S(1)} %get-tuple-element.10), custom_call_target="InvertDiagBlocksLowerTriangular" | custom-call | tf_op jit(solution)/shard_map/triangular_solve | solution.py:63
  406.6 2.2 fusion.27
  410.3 2.6 convolution_subtract_fusion.2
  414.5 2.8 convolution_subtract_fusion.1
  418.7 3.5 convolution_subtract_fusion.3
  423.7 9.1 %fusion.41 = f32[128,2048]{1,0:T(8,128)} fusion(f32[1024,2048]{1,0:T(8,128)} %all-gather.3.cloned.1.call-done, f32[1024,1024]{1,0:T(8,128)} %convolution_dynamic-update-slice_fusion, s32[]{:T(128)S(6)} %select_n.35), kind=kOutput, calls=%fused_computation.68 | convolution fusion | flops 3221225472 | bytes 9961476 | tf_op jit(solution)/shard_map/dot_general | solution.py:32
  435.5 5.2 fusion.97
  440.7 117.1 %all-gather.5.cloned.1.call-done = f32[1024,2048]{1,0:T(8,128)} async-done(((f32[128,2048]{1,0:T(8,128)}), f32[1024,2048]{1,0:T(8,128)}) %all-gather.5.cloned.1.call-update) | async-done | bytes 8388624 | tf_op jit(solution)/shard_map/all_gather | solution.py:70
  557.9 7.3 %fusion.98 = f32[128,2048]{1,0:T(8,128)S(1)} fusion(f32[1024,128]{1,0:T(8,128)S(1)} %fusion.97, f32[1024,2048]{1,0:T(8,128)} %all-gather.5.cloned.1.call-done), kind=kOutput, calls=%fused_computation.198 | convolution fusion | flops 3221225472 | bytes 9961472 | tf_op jit(solution)/shard_map/dot_general | solution.py:38
  565.2 2.2 fusion.5
  (80 shorter events, 51.7 us)
Async XLA Ops:
  7.2 416.5 %all-gather.3.cloned.1.call-start = ((), (), s32[]{:S(2)}) async-start(), calls=%async_computation | async-start | bytes 9437184 | tf_op jit(solution)/shard_map/all_gather | solution.py:69
  26.2 531.7 %all-gather.5.cloned.1.call-start = ((), (), s32[]{:S(2)}) async-start(), calls=%async_computation.1 | async-start | bytes 9437184 | tf_op jit(solution)/shard_map/all_gather | solution.py:70
  80.8 2.0 copy-start
  423.7 10.7 %copy-start.2 = (f32[64]{0:T(128)S(1)}, f32[64]{0:T(128)}, u32[]{:S(2)}) copy-start(f32[64]{0:T(128)} %param.5) | copy-start | bytes 772
  440.7 124.4 %copy-start.1 = (f32[64,2048]{1,0:T(8,128)S(1)}, f32[64,2048]{1,0:T(8,128)}, u32[]{:S(2)}) copy-start(f32[64,2048]{1,0:T(8,128)} %param.3) | copy-start | bytes 1572868
Sparse Core Ops, SparseCore 0:
  26.3 126.6 all-gather.2
  432.9 124.8 all-gather.4
where the time goes:
time: 581 us; the launch traced here: 575 us
  other arithmetic  272 us (47%)
  waiting for transfers between devices  117 us (20%)
  matrix products  85.7 us (15%)
  blocking collectives  45.3 us (8%)
  local copies, waits for them, and re-layouts  34.5 us (6%)
  between operations  20.1 us (3%)
    another operation x30, other arithmetic, body(): diag_full = jnp.linalg.cholesky(diag_block)  172 us
    all_gather x1, waiting for transfers between devices, body(): lax.all_gather(panel_tile, 'col', axis=0, tiled=True)  117 us
    another operation x3, other arithmetic, body(): lax.linalg.triangular_solve(diag_full, identity, left_side=True, lower=True)  85.4 us
    all_gather x1, blocking collectives, body(): all_panel = lax.all_gather(panel_points, 'col', axis=1, tiled=True)  32.4 us
    another operation x15, matrix products, body(): lax.linalg.triangular_solve(diag_full, identity, left_side=True, lower=True)  28.1 us
    another operation x14, matrix products, body(): diag_full = jnp.linalg.cholesky(diag_block)  23.6 us
    another operation x24, local copies, waits for them, and re-layouts  23 us
    dot_general x2, matrix products, times_left(): jnp.dot(matrix, pieces, precision=lax.Precision.HIGHEST, preferred_elemen...  14.3 us
  transfers between devices with their start and end apart: 2, of which 1 were waited for; matrix products, arithmetic and copies ran while one was open for 64% of the time, Pallas kernels for 0%

commit v1 on v0

v1 whole, which is shorter than its diff:
```python
import functools

import jax
import jax.numpy as jnp
from jax import lax
from jax.experimental import pallas as pl
from jax.experimental.pallas import tpu as pltpu
from jax.sharding import PartitionSpec as P

RIDGE = 0.5
BLK = 128
TILE = 256
F32 = jnp.float32
BF16 = jnp.bfloat16


def gather_kernel(n_row, n_col, root, pan_ref, look_ref, g_ref, lk_ref, send, recv, lsend, lrecv, own):
    row = lax.axis_index("row")
    col = lax.axis_index("col")
    barrier = pltpu.get_barrier_semaphore()
    for d in range(1, n_col):
        pl.semaphore_signal(
            barrier, inc=1, device_id=(row, lax.rem(col + d, n_col)), device_id_type=pl.DeviceIdType.MESH
        )
    for d in range(1, n_row):
        pl.semaphore_signal(
            barrier, inc=1, device_id=(lax.rem(row + d, n_row), col), device_id_type=pl.DeviceIdType.MESH
        )
    pl.semaphore_wait(barrier, n_col + n_row - 2)

    def panel_copy(d):
        return pltpu.make_async_remote_copy(
            src_ref=pan_ref,
            dst_ref=g_ref.at[col],
            send_sem=send.at[d],
            recv_sem=recv.at[d],
            device_id=(row, lax.rem(col + d, n_col)),
            device_id_type=pl.DeviceIdType.MESH,
        )

    def panel_arrival(d):
        return pltpu.make_async_remote_copy(
            src_ref=pan_ref,
            dst_ref=g_ref.at[lax.rem(col + n_col - d, n_col)],
            send_sem=send.at[d],
            recv_sem=recv.at[d],
            device_id=(row, lax.rem(col + d, n_col)),
            device_id_type=pl.DeviceIdType.MESH,
        )

    def look_copy(d):
        return pltpu.make_async_remote_copy(
            src_ref=look_ref,
            dst_ref=lk_ref,
            send_sem=lsend.at[d],
            recv_sem=lrecv,
            device_id=(lax.rem(row + d, n_row), col),
            device_id_type=pl.DeviceIdType.MESH,
        )

    @pl.when(row == root)
    def _():
        for d in range(1, n_row):
            look_copy(d).start()

    for d in range(1, n_col):
        panel_copy(d).start()
    mine = pltpu.make_async_copy(pan_ref, g_ref.at[col], own.at[0])
    mine.start()

    @pl.when(row == root)
    def _():
        keep = pltpu.make_async_copy(look_ref, lk_ref, own.at[1])
        keep.start()
        keep.wait()
        for d in range(1, n_row):
            look_copy(d).wait_send()

    @pl.when(row != root)
    def _():
        look_copy(1).wait_recv()

    mine.wait()
    for d in range(1, n_col):
        panel_copy(d).wait_send()
        panel_arrival(d).wait_recv()


def gather_points(panel_points, local_look, n_row, n_col, root):
    feats, share = panel_points.shape
    vmem = pl.BlockSpec(memory_space=pltpu.VMEM)
    return pl.pallas_call(
        functools.partial(gather_kernel, n_row, n_col, root),
        out_shape=(
            jax.ShapeDtypeStruct((n_col, feats, share), F32),
            jax.ShapeDtypeStruct((feats, share), F32),
        ),
        in_specs=[vmem, vmem],
        out_specs=(vmem, vmem),
        scratch_shapes=[
            pltpu.SemaphoreType.DMA((n_col,)),
            pltpu.SemaphoreType.DMA((n_col,)),
            pltpu.SemaphoreType.DMA((n_row,)),
            pltpu.SemaphoreType.DMA,
            pltpu.SemaphoreType.DMA((2,)),
        ],
        compiler_params=pltpu.CompilerParams(collective_id=0, has_side_effects=True),
        name="gather_points",
    )(panel_points, local_look)


def split(x):
    hi = x.astype(BF16)
    return hi, (x - hi.astype(F32)).astype(BF16)


def parts3(x):
    a = x.astype(BF16).astype(F32)
    b = (x - a).astype(BF16).astype(F32)
    return a, b, (x - a) - b


def dot(a, b):
    return jnp.dot(a, b, preferred_element_type=F32)


def dot_t(a, b):
    return lax.dot_general(a, b, (((0,), (0,)), ((), ())), preferred_element_type=F32)


def product(mul, ah, al, bh, bl):
    return mul(ah, bh) + (mul(ah, bl) + mul(al, bh))


def stacked(points, scales, left):
    feats, n = points.shape
    weighted = points * scales
    norm = jnp.sum(weighted * points, axis=0, keepdims=True)
    main = 2.0 * weighted if left else points
    hi = main.astype(BF16).astype(F32)
    lo = main - hi
    n0, n1, n2 = (jnp.broadcast_to(-p, (feats, n)) for p in parts3(norm))
    place = lax.broadcasted_iota(jnp.int32, (feats, n), 0)
    first = 0 if left else 3
    ones = jnp.where((place >= 3 - first) & (place < 6 - first), 1.0, 0.0)
    tail = jnp.where(
        place == first, n0, jnp.where(place == first + 1, n1, jnp.where(place == first + 2, n2, ones))
    )
    blocks = [hi, lo, hi, tail] if left else [hi, hi, lo, tail]
    return jnp.concatenate(blocks, axis=0)


def lanes(x, c):
    return jnp.broadcast_to(x[:, c : c + 1], (8, BLK))


def rows(x, j):
    return jnp.broadcast_to(x[j : j + 1, :], (8, BLK))


def reciprocal(p):
    q = pl.reciprocal(p, approx=True)
    e = 1.0 - p * q
    return q + q * (e + e * e)


def factor_block(block):
    n = BLK // 8
    sub = lax.broadcasted_iota(jnp.int32, (8, BLK), 0)
    lane = lax.broadcasted_iota(jnp.int32, (8, BLK), 1)
    t = [block[8 * r : 8 * r + 8, :] for r in range(n)]
    s = [jnp.where(lane == sub + 8 * r, 1.0, 0.0).astype(F32) for r in range(n)]
    for k in range(n):
        top, side = t[k], s[k]
        v = [lanes(top, 8 * k + j) for j in range(8)]
        mult = []
        diag = jnp.ones((8, BLK), F32)
        for j in range(8):
            across = [rows(v[m], j) for m in range(8)]
            p = across[j]
            q = reciprocal(p)
            vj = v[j]
            mult.append(jnp.where(sub > j, vj * q, 0.0))
            diag = jnp.where(sub == j, p, diag)
            vp = jnp.where(sub == j, vj - 1.0, vj)
            unit = jnp.where(sub == j, 1.0, 0.0)
            v = [unit - vp * q if m == j else v[m] - (vp * across[m]) * q for m in range(8)]
        wt = functools.reduce(jnp.add, [v[j] * rows(top, j) for j in range(8)])
        ws = functools.reduce(jnp.add, [v[j] * rows(side, j) for j in range(8)])
        wtr = [rows(wt, j) for j in range(8)]
        wsr = [rows(ws, j) for j in range(8)]
        for r in range(k + 1, n):
            c = [lanes(t[r], 8 * k + j) for j in range(8)]
            t[r] = t[r] - functools.reduce(jnp.add, [c[j] * wtr[j] for j in range(8)])
            s[r] = s[r] - functools.reduce(jnp.add, [c[j] * wsr[j] for j in range(8)])
        for j in range(7):
            top = top - mult[j] * rows(top, j)
            side = side - mult[j] * rows(side, j)
        root = lax.rsqrt(diag)
        root = root * (1.5 - 0.5 * diag * root * root)
        t[k] = jnp.where(lane >= sub + 8 * k, top * root, 0.0)
        s[k] = side * root
    return jnp.concatenate(t, axis=0), jnp.concatenate(s, axis=0)


def panel_kernel(
    share, pan_ref, look_ref, rows_ref, sc_ref, u_out, panel_out, ahead_out,
    lhs, a, uh, ul, ih, il, work, y, yh, yl, zh, zl,
):
    b = pan_ref.shape[1]
    n_blk = b // BLK
    wide = b + BLK
    col = lax.axis_index("col")
    first = col * share
    home = first // BLK
    scales = sc_ref[...]
    lhs[...] = stacked(pan_ref[...], scales, True).T.astype(BF16)
    look_lhs = stacked(look_ref[...], scales, True).T.astype(BF16)

    def entries(pts):
        return jnp.exp(dot(lhs[...], stacked(pts, scales, False).astype(BF16)))

    for c in range(0, b, TILE):
        at_row = lax.broadcasted_iota(jnp.int32, (b, TILE), 0)
        at_col = lax.broadcasted_iota(jnp.int32, (b, TILE), 1) + c
        a[:, c : c + TILE] = entries(pan_ref[:, c : c + TILE]) + jnp.where(at_row == at_col, RIDGE, 0.0)
    a[:, b:wide] = entries(look_ref[...])

    @pl.loop(0, n_blk)
    def _(kb):
        o = pl.multiple_of(kb * BLK, BLK)
        for i in range(n_blk):

            @pl.when(kb == i)
            def _(i=i):
                s = i * BLK
                cur = a[s : s + BLK, s:wide]
                if i > 0:
                    cur = cur - product(
                        dot_t, uh[:s, s : s + BLK], ul[:s, s : s + BLK], uh[:s, s:wide], ul[:s, s:wide]
                    )
                work[:, :BLK] = cur[:, :BLK]
                a[s : s + BLK, s:wide] = cur

        upper, inverse = factor_block(work[:, :BLK])
        inv_h, inv_l = split(inverse)
        ih[pl.ds(o, BLK), :] = inv_h
        il[pl.ds(o, BLK), :] = inv_l
        for i in range(n_blk):

            @pl.when(kb == i)
            def _(i=i):
                s = i * BLK
                rest = a[s : s + BLK, s + BLK : wide]
                rh, rl = split(rest)
                done = product(dot, inv_h, inv_l, rh, rl)
                a[s : s + BLK, s + BLK : wide] = done
                dh, dl = split(done)
                uh[s : s + BLK, s + BLK : wide] = dh
                ul[s : s + BLK, s + BLK : wide] = dl

        a[pl.ds(o, BLK), pl.ds(o, BLK)] = upper

    at_row = lax.broadcasted_iota(jnp.int32, (BLK, BLK), 0)
    at_col = lax.broadcasted_iota(jnp.int32, (BLK, BLK), 1)
    unit = jnp.where(at_row == at_col, 1.0, 0.0).astype(F32)
    for i in reversed(range(n_blk)):
        s = i * BLK
        right = jnp.concatenate([jnp.where(home == i, unit, 0.0), a[s : s + BLK, b:wide]], axis=1)
        if i < n_blk - 1:
            e = s + BLK
            right = right - product(dot, uh[s:e, e:b], ul[s:e, e:b], yh[e:, :], yl[e:, :])
        rh, rl = split(right)
        done = product(dot_t, ih[s : s + BLK, :], il[s : s + BLK, :], rh, rl)
        y[s : s + BLK, :] = done
        dh, dl = split(done)
        yh[s : s + BLK, :] = dh
        yl[s : s + BLK, :] = dl
    th, tl = split(y[...].T)
    zh[...] = th
    zl[...] = tl

    inner = pl.multiple_of(lax.rem(first, BLK), min(share, BLK))

    @pl.loop(0, rows_ref.shape[1] // TILE)
    def _(step):
        at = pl.ds(pl.multiple_of(step * TILE, TILE), TILE)
        pts = stacked(rows_ref[:, at], scales, False).astype(BF16)
        kh, kl = split(jnp.exp(dot(lhs[...], pts)))
        both = product(dot, zh[...], zl[...], kh, kl)
        ahead = jnp.exp(dot(look_lhs, pts)) - both[BLK:, :]
        if share == BLK:
            panel_out[:, at] = both[:BLK, :]
            ahead_out[:, at] = ahead
        else:
            work[:, :TILE] = both[:BLK, :]
            panel_out[:, at] = work[pl.ds(inner, share), :TILE]
            ahead_out[:, at] = ahead[:share, :]

    u_rows = u_out.shape[1]
    u_out[...] = a[
        pl.ds(pl.multiple_of(first, share), share),
        pl.ds(pl.multiple_of(lax.axis_index("row") * u_rows, BLK), u_rows),
    ]


def panel_step(panel, look, row_points, scales, share, row_share):
    feats, b = panel.shape
    rows_dev = row_points.shape[1]
    wide = b + BLK
    vmem = pl.BlockSpec(memory_space=pltpu.VMEM)
    return pl.pallas_call(
        functools.partial(panel_kernel, share),
        out_shape=(
            jax.ShapeDtypeStruct((share, row_share), F32),
            jax.ShapeDtypeStruct((share, rows_dev), F32),
            jax.ShapeDtypeStruct((share, rows_dev), F32),
        ),
        in_specs=[vmem] * 4,
        out_specs=(vmem,) * 3,
        scratch_shapes=[
            pltpu.VMEM((b, 4 * feats), BF16),
            pltpu.VMEM((b, wide), F32),
            pltpu.VMEM((b, wide), BF16),
            pltpu.VMEM((b, wide), BF16),
            pltpu.VMEM((b, BLK), BF16),
            pltpu.VMEM((b, BLK), BF16),
            pltpu.VMEM((BLK, TILE), F32),
            pltpu.VMEM((b, 2 * BLK), F32),
            pltpu.VMEM((b, 2 * BLK), BF16),
            pltpu.VMEM((b, 2 * BLK), BF16),
            pltpu.VMEM((2 * BLK, b), BF16),
            pltpu.VMEM((2 * BLK, b), BF16),
        ],
        compiler_params=pltpu.CompilerParams(vmem_limit_bytes=48 * 1024 * 1024),
        name="panel_step",
    )(panel, look, row_points, scales[:, None])


def body(row_points, panel_points, scales):
    n_col = lax.axis_size("col")
    n_row = lax.axis_size("row")
    col_index = lax.axis_index("col")
    row_index = lax.axis_index("row")
    feats, share = panel_points.shape
    b = share * n_col
    row_share = b // n_row
    rows_dev = row_points.shape[1]
    assert b <= rows_dev and BLK % share == 0
    first_col = col_index * share
    local_look = lax.dynamic_slice_in_dim(row_points, first_col, share, 1)
    gathered, look = gather_points(panel_points, local_look, n_row, n_col, 0)
    panel = jnp.transpose(gathered, (1, 0, 2)).reshape(feats, b)
    look = jnp.pad(look, ((0, 0), (0, BLK - share)))
    u_tile, panel_tile, updated = panel_step(panel, look, row_points, scales, share, row_share)
    at_row = lax.broadcasted_iota(jnp.int32, (row_share, share), 0) + row_index * row_share
    at_col = lax.broadcasted_iota(jnp.int32, (row_share, share), 1) + first_col
    diag_tile = jnp.where(at_row >= at_col, u_tile.T, 0.0)
    return (diag_tile, panel_tile, updated)


def solution(mesh):
    return jax.shard_map(
        body,
        mesh=mesh,
        in_specs=(P(None, "row"), P(None, "col"), P()),
        out_specs=(P("row", "col"), P("col", "row"), P("col", "row")),
        check_vma=False,
    )
```

time: 581 us -> 84.8 us (0.15); the launches traced: 575 us -> 84.5 us
  other arithmetic: 272 us -> 0.09 us
  waiting for transfers between devices: 117 us -> 0 us
  matrix products: 85.7 us -> 0 us
  Pallas kernels: 0 us -> 79.8 us
  blocking collectives: 45.3 us -> 0 us
  local copies, waits for them, and re-layouts: 34.5 us -> 3.91 us
  between operations: 20.1 us -> 0.69 us
    another operation x33 -> x0, other arithmetic: 257 us -> none  [the longest x30 172 us: body(): diag_full = jnp.linalg.cholesky(diag_block)]
    all_gather x2 -> x0, waiting for transfers between devices: 117 us -> none  [the longest x1 117 us: body(): lax.all_gather(panel_tile, 'col', axis=0, tiled=True)]
    pallas_call x0 -> x2, Pallas kernels: none -> 79.8 us  [the longest x1 66.8 us: panel_step(): pl.pallas_call(functools.partial(panel_kernel, share), out_shape=(jax.Sha...]
    another operation x29 -> x0, matrix products: 51.7 us -> none  [the longest x15 28.1 us: body(): lax.linalg.triangular_solve(diag_full, identity, left_side=True, lower=True)]
    dot_general x7 -> x0, matrix products: 34 us -> none  [the longest x2 14.3 us: times_left(): jnp.dot(matrix, pieces, precision=lax.Precision.HIGHEST, preferred_elemen...]
    all_gather x1 -> x0, blocking collectives: 32.4 us -> none  [body(): all_panel = lax.all_gather(panel_points, 'col', axis=1, tiled=True)]
    another operation x33 -> x0, local copies, waits for them, and re-layouts: 25.5 us -> none
    psum x1 -> x0, blocking collectives: 12.9 us -> none  [spread(): return lax.psum(block, axis)]
  transfers between devices with their start and end apart: 2 -> 0, of which waited for: 1 -> 0; matrix products, arithmetic and copies ran while one was open for 64% -> 0% of each run, Pallas kernels for 0% -> 0%
where the time goes in v1:
time: 84.8 us; the launch traced here: 84.5 us
  Pallas kernels  79.8 us (94%)
  local copies, waits for them, and re-layouts  3.91 us (5%)
    pallas_call x1, Pallas kernels, panel_step(): pl.pallas_call(functools.partial(panel_kernel, share), out_shape=(jax.Sha...  66.8 us
    pallas_call x1, Pallas kernels, gather_points(): pl.pallas_call(functools.partial(gather_kernel, n_row, n_col, root), out_...  12.9 us

profile of v1, /device:TPU:0, one launch (start us, length us, event | category | flops | bytes accessed | tf_op | source)
XLA Modules:
  0.0 84.5 jit_solution(393520934566837128)
XLA Ops:
  0.6 0.0 copy-start
  0.6 1.4 %constant_dynamic-slice_fusion.look_ref = f32[64,128]{1,0:T(8,128)} fusion(f32[64,2048]{1,0:T(8,128)} %rows_ref.1, s32[]{:T(128)S(6)} %select_n.7), kind=kLoop, calls=%fused_computation.4 | loop fusion | bytes 65540 | tf_op jit(solution)/shard_map/dynamic_slice | solution.py:351
  2.1 12.9 %gather_points.1 = (f32[8,64,128]{2,1,0:T(8,128)}, f32[64,128]{1,0:T(8,128)}) custom-call(f32[64,128]{1,0:T(8,128)} %pan_ref.1, f32[64,128]{1,0:T(8,128)} %constant_dynamic-slice_fusion.look_ref), custom_call_target="tpu_custom_call" | custom-call | tf_op jit(solution)/shard_map/gather_points/pallas_call | solution.py:92
  15.0 0.0 copy-start.2
  15.0 1.0 %copy_bitcast_fusion.pan_ref = f32[64,1024]{1,0:T(8,128)S(1)} fusion(f32[8,64,128]{2,1,0:T(8,128)} %get-tuple-element.8), kind=kLoop, calls=%fused_computation | loop fusion | bytes 524288 | tf_op jit(solution)/shard_map/reshape | solution.py:353
  16.0 0.0 copy-start.1
  16.0 0.0 copy-done.2
  16.0 0.1 copy.7.sc_ref
  16.1 0.0 copy-done
  16.1 0.6 copy-done.1
  16.8 66.8 %panel_step.1 = (f32[128,256]{1,0:T(8,128)S(1)}, f32[128,2048]{1,0:T(8,128)}, f32[128,2048]{1,0:T(8,128)}) custom-call(f32[64,1024]{1,0:T(8,128)S(1)} %copy_bitcast_fusion.pan_ref, f32[64,128]{1,0:T(8,128)S(1)} %copy-done.1, f32[64,2048]{1,0:T(8,128)S(1)} %copy-done, f32[64,1]{1,0:T(8,128)S(1)} %copy.7.sc_ref), custom_call_target="tpu_custom_call" | custom-call | tf_op jit(solution)/shard_map/panel_step/pallas_call | solution.py:312
  83.6 0.1 bitcast_select_fusion
  83.7 0.8 copy.8
  (2 shorter events, 0.0 us)
Async XLA Ops:
  0.6 15.5 %copy-start = (f32[64,2048]{1,0:T(8,128)S(1)}, f32[64,2048]{1,0:T(8,128)}, u32[]{:S(2)}) copy-start(f32[64,2048]{1,0:T(8,128)} %rows_ref.1) | copy-start | bytes 1572868
  15.0 1.0 %copy-start.2 = (f32[64]{0:T(128)S(1)}, f32[64]{0:T(128)}, u32[]{:S(2)}) copy-start(f32[64]{0:T(128)} %param.5) | copy-start | bytes 772
  16.0 0.8 copy-start.1

commit v2 on v1

--- a/solution.py
+++ b/solution.py
@@ -17,6 +17,15 @@
 def gather_kernel(n_row, n_col, root, pan_ref, look_ref, g_ref, lk_ref, send, recv, lsend, lrecv, own):
     row = lax.axis_index("row")
     col = lax.axis_index("col")
+    share = pan_ref.shape[1]
+    aligned = share % BLK == 0
+
+    def slot(c):
+        if aligned:
+            return g_ref.at[:, pl.ds(pl.multiple_of(c * share, share), share)]
+        return g_ref.at[c]
+
+    look_src = look_ref.at[:, pl.ds(pl.multiple_of(col * share, share), share)] if aligned else look_ref
     barrier = pltpu.get_barrier_semaphore()
     for d in range(1, n_col):
         pl.semaphore_signal(
@@ -31,7 +40,7 @@
     def panel_copy(d):
         return pltpu.make_async_remote_copy(
             src_ref=pan_ref,
-            dst_ref=g_ref.at[col],
+            dst_ref=slot(col),
             send_sem=send.at[d],
             recv_sem=recv.at[d],
             device_id=(row, lax.rem(col + d, n_col)),
@@ -41,7 +50,7 @@
     def panel_arrival(d):
         return pltpu.make_async_remote_copy(
             src_ref=pan_ref,
-            dst_ref=g_ref.at[lax.rem(col + n_col - d, n_col)],
+            dst_ref=slot(lax.rem(col + n_col - d, n_col)),
             send_sem=send.at[d],
             recv_sem=recv.at[d],
             device_id=(row, lax.rem(col + d, n_col)),
@@ -50,7 +59,7 @@
 
     def look_copy(d):
         return pltpu.make_async_remote_copy(
-            src_ref=look_ref,
+            src_ref=look_src,
             dst_ref=lk_ref,
             send_sem=lsend.at[d],
             recv_sem=lrecv,
@@ -65,12 +74,12 @@
 
     for d in range(1, n_col):
         panel_copy(d).start()
-    mine = pltpu.make_async_copy(pan_ref, g_ref.at[col], own.at[0])
+    mine = pltpu.make_async_copy(pan_ref, slot(col), own.at[0])
     mine.start()
 
     @pl.when(row == root)
     def _():
-        keep = pltpu.make_async_copy(look_ref, lk_ref, own.at[1])
+        keep = pltpu.make_async_copy(look_src, lk_ref, own.at[1])
         keep.start()
         keep.wait()
         for d in range(1, n_row):
@@ -92,10 +101,10 @@
     return pl.pallas_call(
         functools.partial(gather_kernel, n_row, n_col, root),
         out_shape=(
-            jax.ShapeDtypeStruct((n_col, feats, share), F32),
+            jax.ShapeDtypeStruct((feats, n_col * share) if share % BLK == 0 else (n_col, feats, share), F32),
             jax.ShapeDtypeStruct((feats, share), F32),
         ),
-        in_specs=[vmem, vmem],
+        in_specs=[vmem, pl.BlockSpec(memory_space=pl.ANY) if share % BLK == 0 else vmem],
         out_specs=(vmem, vmem),
         scratch_shapes=[
             pltpu.SemaphoreType.DMA((n_col,)),
@@ -159,9 +168,13 @@
 
 
 def reciprocal(p):
-    q = pl.reciprocal(p, approx=True)
-    e = 1.0 - p * q
-    return q + q * (e + e * e)
+    return pl.reciprocal(p, approx=True)
+
+
+def total(terms):
+    while len(terms) > 1:
+        terms = [terms[i] + terms[i + 1] for i in range(0, len(terms), 2)]
+    return terms[0]
 
 
 def factor_block(block):
@@ -175,29 +188,41 @@
         v = [lanes(top, 8 * k + j) for j in range(8)]
         mult = []
         diag = jnp.ones((8, BLK), F32)
-        for j in range(8):
-            across = [rows(v[m], j) for m in range(8)]
-            p = across[j]
-            q = reciprocal(p)
-            vj = v[j]
-            mult.append(jnp.where(sub > j, vj * q, 0.0))
-            diag = jnp.where(sub == j, p, diag)
-            vp = jnp.where(sub == j, vj - 1.0, vj)
-            unit = jnp.where(sub == j, 1.0, 0.0)
-            v = [unit - vp * q if m == j else v[m] - (vp * across[m]) * q for m in range(8)]
-        wt = functools.reduce(jnp.add, [v[j] * rows(top, j) for j in range(8)])
-        ws = functools.reduce(jnp.add, [v[j] * rows(side, j) for j in range(8)])
+        for x in range(0, 8, 2):
+            z = x + 1
+            f = [rows(v[m], x) for m in range(8)]
+            g = [rows(v[m], z) for m in range(8)]
+            pa, pb, pc = f[x], f[z], g[z]
+            det = pa * pc - pb * pb
+            q = reciprocal(det)
+            qa = reciprocal(pa)
+            mult.append(jnp.where(sub > x, v[x] * qa, 0.0))
+            mult.append(jnp.where(sub > z, (v[z] - v[x] * (pb * qa)) * (pa * q), 0.0))
+            diag = jnp.where(sub == x, pa, jnp.where(sub == z, det * qa, diag))
+            vx = jnp.where(sub == x, v[x] - 1.0, v[x])
+            vz = jnp.where(sub == z, v[z] - 1.0, v[z])
+            hx = pc * vx - pb * vz
+            hz = pa * vz - pb * vx
+            v = [
+                jnp.where(sub == x, 1.0, 0.0) - hx * q
+                if m == x
+                else jnp.where(sub == z, 1.0, 0.0) - hz * q
+                if m == z
+                else v[m] - (hx * f[m] + hz * g[m]) * q
+                for m in range(8)
+            ]
+        wt = total([v[j] * rows(top, j) for j in range(8)])
+        ws = total([v[j] * rows(side, j) for j in range(8)])
         wtr = [rows(wt, j) for j in range(8)]
         wsr = [rows(ws, j) for j in range(8)]
         for r in range(k + 1, n):
             c = [lanes(t[r], 8 * k + j) for j in range(8)]
-            t[r] = t[r] - functools.reduce(jnp.add, [c[j] * wtr[j] for j in range(8)])
-            s[r] = s[r] - functools.reduce(jnp.add, [c[j] * wsr[j] for j in range(8)])
+            t[r] = t[r] - total([c[j] * wtr[j] for j in range(8)])
+            s[r] = s[r] - total([c[j] * wsr[j] for j in range(8)])
         for j in range(7):
             top = top - mult[j] * rows(top, j)
             side = side - mult[j] * rows(side, j)
         root = lax.rsqrt(diag)
-        root = root * (1.5 - 0.5 * diag * root * root)
         t[k] = jnp.where(lane >= sub + 8 * k, top * root, 0.0)
         s[k] = side * root
     return jnp.concatenate(t, axis=0), jnp.concatenate(s, axis=0)
@@ -217,49 +242,39 @@
     lhs[...] = stacked(pan_ref[...], scales, True).T.astype(BF16)
     look_lhs = stacked(look_ref[...], scales, True).T.astype(BF16)
 
-    def entries(pts):
-        return jnp.exp(dot(lhs[...], stacked(pts, scales, False).astype(BF16)))
+    def entries(pts, e):
+        return jnp.exp(dot(lhs[:e, :], stacked(pts, scales, False).astype(BF16)))
 
     for c in range(0, b, TILE):
-        at_row = lax.broadcasted_iota(jnp.int32, (b, TILE), 0)
-        at_col = lax.broadcasted_iota(jnp.int32, (b, TILE), 1) + c
-        a[:, c : c + TILE] = entries(pan_ref[:, c : c + TILE]) + jnp.where(at_row == at_col, RIDGE, 0.0)
-    a[:, b:wide] = entries(look_ref[...])
-
-    @pl.loop(0, n_blk)
-    def _(kb):
-        o = pl.multiple_of(kb * BLK, BLK)
-        for i in range(n_blk):
-
-            @pl.when(kb == i)
-            def _(i=i):
-                s = i * BLK
-                cur = a[s : s + BLK, s:wide]
-                if i > 0:
-                    cur = cur - product(
-                        dot_t, uh[:s, s : s + BLK], ul[:s, s : s + BLK], uh[:s, s:wide], ul[:s, s:wide]
-                    )
-                work[:, :BLK] = cur[:, :BLK]
-                a[s : s + BLK, s:wide] = cur
-
-        upper, inverse = factor_block(work[:, :BLK])
+        e = c + TILE
+        at_row = lax.broadcasted_iota(jnp.int32, (e, TILE), 0)
+        at_col = lax.broadcasted_iota(jnp.int32, (e, TILE), 1) + c
+        a[:e, c:e] = entries(pan_ref[:, c:e], e) + jnp.where(at_row == at_col, RIDGE, 0.0)
+    a[:, b:wide] = entries(look_ref[...], b)
+
+    for i in range(n_blk):
+        s = i * BLK
+        e = s + BLK
+
+        def current(lo, hi, s=s, e=e):
+            cur = a[s:e, lo:hi]
+            if s > 0:
+                cur = cur - product(dot_t, uh[:s, s:e], ul[:s, s:e], uh[:s, lo:hi], ul[:s, lo:hi])
+            return cur
+
+        upper, inverse = factor_block(current(s, e))
+        a[s:e, s:e] = upper
         inv_h, inv_l = split(inverse)
-        ih[pl.ds(o, BLK), :] = inv_h
-        il[pl.ds(o, BLK), :] = inv_l
-        for i in range(n_blk):
-
-            @pl.when(kb == i)
-            def _(i=i):
-                s = i * BLK
-                rest = a[s : s + BLK, s + BLK : wide]
-                rh, rl = split(rest)
+        ih[s:e, :] = inv_h
+        il[s:e, :] = inv_l
+        for lo, hi in ((e, e + BLK), (e + BLK, wide)):
+            if lo < hi:
+                rh, rl = split(current(lo, hi))
                 done = product(dot, inv_h, inv_l, rh, rl)
-                a[s : s + BLK, s + BLK : wide] = done
+                a[s:e, lo:hi] = done
                 dh, dl = split(done)
-                uh[s : s + BLK, s + BLK : wide] = dh
-                ul[s : s + BLK, s + BLK : wide] = dl
-
-        a[pl.ds(o, BLK), pl.ds(o, BLK)] = upper
+                uh[s:e, lo:hi] = dh
+                ul[s:e, lo:hi] = dl
 
     at_row = lax.broadcasted_iota(jnp.int32, (BLK, BLK), 0)
     at_col = lax.broadcasted_iota(jnp.int32, (BLK, BLK), 1)
@@ -297,11 +312,15 @@
             panel_out[:, at] = work[pl.ds(inner, share), :TILE]
             ahead_out[:, at] = ahead[:share, :]
 
-    u_rows = u_out.shape[1]
-    u_out[...] = a[
-        pl.ds(pl.multiple_of(first, share), share),
-        pl.ds(pl.multiple_of(lax.axis_index("row") * u_rows, BLK), u_rows),
-    ]
+    u_rows = u_out.shape[0] if share == BLK else u_out.shape[1]
+    u_first = pl.multiple_of(lax.axis_index("row") * u_rows, BLK)
+    u_tile = a[pl.ds(pl.multiple_of(first, share), share), pl.ds(u_first, u_rows)]
+    if share == BLK:
+        at_row = lax.broadcasted_iota(jnp.int32, (u_rows, share), 0) + u_first
+        at_col = lax.broadcasted_iota(jnp.int32, (u_rows, share), 1) + first
+        u_out[...] = jnp.where(at_row >= at_col, u_tile.T, 0.0)
+    else:
+        u_out[...] = u_tile
 
 
 def panel_step(panel, look, row_points, scales, share, row_share):
@@ -312,7 +331,7 @@
     return pl.pallas_call(
         functools.partial(panel_kernel, share),
         out_shape=(
-            jax.ShapeDtypeStruct((share, row_share), F32),
+            jax.ShapeDtypeStruct((row_share, share) if share == BLK else (share, row_share), F32),
             jax.ShapeDtypeStruct((share, rows_dev), F32),
             jax.ShapeDtypeStruct((share, rows_dev), F32),
         ),
@@ -348,6 +367,9 @@
     rows_dev = row_points.shape[1]
     assert b <= rows_dev and BLK % share == 0
     first_col = col_index * share
+    if share == BLK:
+        panel, look = gather_points(panel_points, row_points, n_row, n_col, 0)
+        return panel_step(panel, look, row_points, scales, share, row_share)
     local_look = lax.dynamic_slice_in_dim(row_points, first_col, share, 1)
     gathered, look = gather_points(panel_points, local_look, n_row, n_col, 0)
     panel = jnp.transpose(gathered, (1, 0, 2)).reshape(feats, b)

time: 84.8 us -> 68.7 us (0.81)
  Pallas kernels: 79.8 us -> 65.2 us
  local copies, waits for them, and re-layouts: 3.91 us -> 2.51 us
    pallas_call x1, Pallas kernels: 66.8 us -> 52.3 us  [panel_step(): pl.pallas_call(functools.partial(panel_kernel, share), out_shape=(jax.Sha...]
    dynamic_slice x1 -> x0, local copies, waits for them, and re-layouts: 1.43 us -> none  [body(): local_look = lax.dynamic_slice_in_dim(row_points, first_col, share, 1)]
    reshape x1 -> x0, local copies, waits for them, and re-layouts: 0.97 us -> none  [body(): panel = jnp.transpose(gathered, (1, 0, 2)).reshape(feats, b)]
    unnamed x7 -> x6, local copies, waits for them, and re-layouts: 1.41 us -> 1.71 us
where the time goes in v2:
time: 68.7 us; the launch traced here: 68.4 us
  Pallas kernels  65.2 us (95%)
  local copies, waits for them, and re-layouts  2.51 us (4%)
    pallas_call x1, Pallas kernels, panel_step(): pl.pallas_call(functools.partial(panel_kernel, share), out_shape=(jax.Sha...  52.3 us
    pallas_call x1, Pallas kernels, gather_points(): pl.pallas_call(functools.partial(gather_kernel, n_row, n_col, root), out_...  12.9 us
    unnamed x6, local copies, waits for them, and re-layouts  1.71 us

profile of v2, /device:TPU:0, one launch (start us, length us, event | category | flops | bytes accessed | tf_op | source)
XLA Modules:
  0.0 68.4 jit_solution(2687465743153339041)
XLA Ops:
  0.6 0.0 copy-start
  0.6 0.8 %copy.6.sc_ref = f32[64,1]{1,0:T(8,128)S(1)} copy(f32[64,1]{0,1:T(1,128)} %bitcast.1) | data formatting | bytes 512 | tf_op jit(solution)/shard_map/broadcast_in_dim | solution.py:356
  1.4 12.9 %gather_points.1 = (f32[64,1024]{1,0:T(8,128)}, f32[64,128]{1,0:T(8,128)}) custom-call(f32[64,128]{1,0:T(8,128)} %pan_ref.1, f32[64,2048]{1,0:T(8,128)} %rows_ref.1), custom_call_target="tpu_custom_call" | custom-call | tf_op jit(solution)/shard_map/gather_points/pallas_call | solution.py:101
  14.4 0.0 copy-done
  14.4 0.0 copy-start.1
  14.4 0.9 %copy-done.1 = f32[64,1024]{1,0:T(8,128)S(1)} copy-done((f32[64,1024]{1,0:T(8,128)S(1)}, f32[64,1024]{1,0:T(8,128)}, u32[]{:S(2)}) %copy-start.1) | copy-done | bytes 262168
  15.3 0.0 copy-start.2
  15.3 0.8 %copy-done.2 = f32[64,128]{1,0:T(8,128)S(1)} copy-done((f32[64,128]{1,0:T(8,128)S(1)}, f32[64,128]{1,0:T(8,128)}, u32[]{:S(2)}) %copy-start.2) | copy-done | bytes 32792
  16.1 52.3 %panel_step.1 = (f32[256,128]{1,0:T(8,128)}, f32[128,2048]{1,0:T(8,128)}, f32[128,2048]{1,0:T(8,128)}) custom-call(f32[64,1024]{1,0:T(8,128)S(1)} %copy-done.1, f32[64,128]{1,0:T(8,128)S(1)} %copy-done.2, f32[64,2048]{1,0:T(8,128)S(1)} %copy-done, f32[64,1]{1,0:T(8,128)S(1)} %copy.6.sc_ref), custom_call_target="tpu_custom_call" | custom-call | tf_op jit(solution)/shard_map/panel_step/pallas_call | solution.py:331
Async XLA Ops:
  0.6 13.7 %copy-start = (f32[64,2048]{1,0:T(8,128)S(1)}, f32[64,2048]{1,0:T(8,128)}, u32[]{:S(2)}) copy-start(f32[64,2048]{1,0:T(8,128)} %rows_ref.1) | copy-start | bytes 1572868
  14.4 1.0 %copy-start.1 = (f32[64,1024]{1,0:T(8,128)S(1)}, f32[64,1024]{1,0:T(8,128)}, u32[]{:S(2)}) copy-start(f32[64,1024]{1,0:T(8,128)} %get-tuple-element.5.pan_ref) | copy-start | bytes 786436
  15.3 0.8 %copy-start.2 = (f32[64,128]{1,0:T(8,128)S(1)}, f32[64,128]{1,0:T(8,128)}, u32[]{:S(2)}) copy-start(f32[64,128]{1,0:T(8,128)} %get-tuple-element.6.look_ref) | copy-start | bytes 98308
